TPU v7x, 128 devices: a whole 4x4x4 slice. The times are simulated.
128 devices in a mesh: wide: 32 (over z, y, core), narrow: 4 (over x).
Axes of the slice: x: 4, y: 4, z: 4, core: 2. Of those that a mesh axis runs over, the one named last changes fastest.
Arguments:
- embeddings: float32 [16384, 1024], P(('wide', 'narrow')), may hold values from -6 to 6
- cluster: int32 [16384], P(('wide', 'narrow')), may hold values from 0 to 63, as said below
- order: int32 [16384], P(('wide', 'narrow')), may hold values from 0 to 511
Outputs:
- best_similarity: float32 [16384], P(('wide', 'narrow'))
Inputs may be any that keep to these rules, and one draw needn't show every extreme that they name: Documents of one cluster have distinct order values. For every k, at most 8 documents of one device lie in clusters k * 2 to k * 2 + 1, and on every device exactly 8 for some k.
All inputs are finite; a program needn't handle non-finite values.
Results may differ from a plain program's by a relative error of at most 0.0013.
Values may be sent and summed in bfloat16 or wider, within the bound.
No kernel may reach another device: no remote copies, remote signals or barrier semaphores. Data moves between devices by JAX's collectives and lax.ppermute only.
A program may use at most 64 MiB of HBM per device.

v0:
```python
import jax
import jax.numpy as jnp
from jax import lax
from jax.experimental import pallas as pl
from jax.experimental.pallas import tpu as pltpu
from jax.sharding import Mesh, PartitionSpec as P

CLUSTERS = 64
SLOTS = 8
CAP = 512
LANES = 128
CORES = 2
CHUNKS = 4
GROUPS = CLUSTERS // CHUNKS
PART = GROUPS * SLOTS
TILES = 33
epsilon = 1e-06

VMEM = 32 * 1024 * 1024
NT = (((1,), (1,)), ((), ()))


def iota(shape, axis):
    return lax.broadcasted_iota(jnp.int32, shape, axis)


def as_bf16(mask):
    return jnp.where(mask, 1.0, 0.0).astype(jnp.bfloat16)


def pack_kernel(rows_hbm, cluster_hbm, order_hbm, out_ref, where_ref, rows_ref, ids_ref, sems):
    docs, width = rows_ref.shape
    cluster_copy = pltpu.make_async_copy(cluster_hbm, ids_ref.at[0], sems.at[0])
    order_copy = pltpu.make_async_copy(order_hbm, ids_ref.at[1], sems.at[1])
    rows_copy = pltpu.make_async_copy(rows_hbm, rows_ref, sems.at[2])
    cluster_copy.start()
    order_copy.start()
    rows_copy.start()
    before = as_bf16(iota((docs, docs), 0) < iota((docs, docs), 1))
    cluster_copy.wait()
    order_copy.wait()
    cluster = ids_ref[0]
    member = iota((CLUSTERS, docs), 0) == cluster
    count = jnp.dot(as_bf16(member), before, preferred_element_type=jnp.float32)
    position = jnp.sum(jnp.where(member, count, 0.0), axis=0, keepdims=True).astype(jnp.int32)
    chip = lax.axis_index("x") * lax.axis_size("zy") + lax.axis_index("zy")
    where_ref[0:1] = cluster
    where_ref[1:2] = chip // CHUNKS * SLOTS + (chip % CHUNKS * 2 + position) % SLOTS
    chunk = cluster % CHUNKS
    start = chunk * PART + cluster // CHUNKS * SLOTS
    line = iota((CHUNKS * PART, docs), 0)
    place = as_bf16(line == start + (chunk * 2 + position) % SLOTS)
    rank = ids_ref[1] - CAP
    high = (rank >> 4).astype(jnp.float32)
    low = (rank & 15).astype(jnp.float32)
    high_line = start + chunk * 2
    marks = jnp.where(line == high_line, high, jnp.where(line == high_line + 1, low, 0.0))
    marks = lax.dot_general(
        marks.astype(jnp.bfloat16),
        as_bf16(iota((LANES, docs), 0) == position),
        NT,
        preferred_element_type=jnp.float32,
    )
    rows_copy.wait()
    rows = rows_ref[...]
    squares = jnp.sum(rows * rows, axis=1, keepdims=True)
    unit = (rows * lax.rsqrt(squares + epsilon)).astype(jnp.bfloat16)
    line = iota((GROUPS, SLOTS, LANES), 1).astype(jnp.float32).astype(jnp.bfloat16)
    carried = None
    for at in range(CHUNKS):
        part = slice(at * PART, (at + 1) * PART)
        packed = jnp.dot(place[part], unit, preferred_element_type=jnp.float32)
        packed = packed.astype(jnp.bfloat16)
        mine = line >= jnp.asarray(at * 2, jnp.bfloat16)
        for lane in range(0, width, LANES):
            tile = packed[:, lane : lane + LANES].reshape(GROUPS, SLOTS, LANES)
            value = tile if carried is None else jnp.where(mine, tile, carried)
            out_ref[:, at * 8 + lane // LANES] = value
            carried = tile
        mark = marks[part].astype(jnp.bfloat16).reshape(GROUPS, SLOTS, LANES)
        carried = jnp.where(mine, mark, carried)
    out_ref[:, TILES - 1] = carried


def unfold(ref):
    slot = iota((GROUPS, SLOTS, LANES), 1)
    lane = iota((GROUPS, SLOTS, LANES), 2)
    rows, ranks = [], []
    for chunk in range(CHUNKS):
        turn = chunk * 2
        tiles = [ref[:, chunk * 8 + i] for i in range(9)]
        if chunk > 0:
            line = slot.astype(jnp.float32).astype(jnp.bfloat16)
            mine = line >= jnp.asarray(turn, jnp.bfloat16)
            data = [jnp.where(mine, x, y) for x, y in zip(tiles[:-1], tiles[1:])]
        else:
            data = tiles[:-1]
        rows.append(jnp.concatenate([x.reshape(PART, LANES) for x in data], axis=1))
        marks = tiles[-1].astype(jnp.float32)
        rank = marks[:, turn : turn + 1] * 16.0 + marks[:, turn + 1 : turn + 2]
        mine = lane == (slot - turn) % SLOTS
        rank = jnp.sum(jnp.where(mine, rank, 0.0), axis=2, keepdims=True)
        ranks.append(jnp.broadcast_to(rank, (GROUPS, SLOTS, LANES)).reshape(PART, LANES))
    return jnp.concatenate(rows, axis=0), jnp.concatenate(ranks, axis=0)


def largest(values):
    return jnp.max(values.reshape(-1, 8, values.shape[1]), axis=0)


def similarities(keys, queries_ref):
    step = 2 * LANES
    for at in range(0, queries_ref.shape[1], step):
        similar = jnp.dot(
            keys, queries_ref[:, at : at + step], preferred_element_type=jnp.float32
        )
        for lane in range(0, step, LANES):
            yield at + lane, similar[:, lane : lane + LANES]


def maxima(keys, key_rank, queries_ref, rank_ref):
    for at, similar in similarities(keys, queries_ref):
        allowed = key_rank < rank_ref[0:1, at : at + LANES]
        yield at, largest(jnp.where(allowed, similar, -1.0))


def first_kernel(early_ref, late_ref, other_ref, queries_ref, rank_ref, best_ref, away_ref):
    core = lax.axis_index("core")

    def turn(rows, ranks):
        queries_ref[...] = rows.T
        rank_ref[...] = ranks.T[0:8]

    @pl.when(core == 0)
    def _():
        turn(*unfold(late_ref))
        keys, key_rank = unfold(other_ref)
        away = jnp.full(key_rank.shape, -1.0, jnp.float32)
        for at, similar in similarities(keys, queries_ref):
            rank = rank_ref[0:1, at : at + LANES]
            best_ref[:, at : at + LANES] = largest(jnp.where(key_rank < rank, similar, -1.0))
            away = jnp.maximum(away, jnp.where(rank < key_rank, similar, -1.0))
        away_ref[...] = largest(away.T)

    @pl.when(core != 0)
    def _():
        rows, ranks = unfold(early_ref)
        turn(rows, ranks)
        for at, best in maxima(rows, ranks, queries_ref, rank_ref):
            best_ref[:, at : at + LANES] = best
        away_ref[...] = jnp.full(away_ref.shape, -1.0, jnp.float32)


def second_kernel(late_ref, queries_ref, rank_ref, first_ref, best_ref):
    core = lax.axis_index("core")

    @pl.when(core == 0)
    def _():
        for at, best in maxima(*unfold(late_ref), queries_ref, rank_ref):
            best_ref[:, at : at + LANES] = jnp.maximum(best, first_ref[:, at : at + LANES])

    @pl.when(core != 0)
    def _():
        best_ref[...] = first_ref[...]


def merge_kernel(best_ref, away_ref, out_ref):
    away = jnp.where(lax.axis_index("core") == 0, -1.0, away_ref[...])
    best = jnp.max(jnp.maximum(best_ref[...], away), axis=0, keepdims=True)
    lines = [best[:, at : at + LANES] for at in range(0, best.shape[1], LANES)]
    lines = jnp.concatenate(lines + lines)
    for at in range(0, CLUSTERS, 8):
        out_ref[at : at + 8] = lines


def unpack_kernel(best_ref, where_ref, out_ref):
    docs = where_ref.shape[1]
    best = jnp.concatenate([best_ref[...], jnp.zeros((LANES - CLUSTERS, LANES), jnp.float32)])
    cluster = jnp.broadcast_to(where_ref[0:1], (LANES, docs))
    by_cluster = jnp.take_along_axis(best.T, cluster, axis=1)
    wanted = iota((LANES, docs), 0) == where_ref[1:2]
    out_ref[...] = jnp.sum(jnp.where(wanted, by_cluster, 0.0), axis=0, keepdims=True)


def call(kernel, out_shape, flops, moved, **more):
    return pl.pallas_call(
        kernel,
        out_shape=out_shape,
        compiler_params=pltpu.CompilerParams(vmem_limit_bytes=VMEM),
        cost_estimate=pl.CostEstimate(flops=flops, bytes_accessed=moved, transcendentals=0),
        **more,
    )


def in_hbm(x):
    return pltpu.with_memory_space_constraint(x, pltpu.HBM)


def per_device(embeddings, cluster, order):
    docs, width = embeddings.shape
    slots = CLUSTERS * SLOTS
    shape = jax.ShapeDtypeStruct
    f32, bf16, i32 = jnp.float32, jnp.bfloat16, jnp.int32
    tiles = (GROUPS, TILES, 8, LANES)
    moved = CLUSTERS * (SLOTS * width + 2 * LANES) * 2
    packed, where = call(
        pack_kernel,
        (shape(tiles, bf16), shape((8, docs), i32)),
        2 * slots * docs * width,
        docs * width * 4 + moved,
        in_specs=[pl.BlockSpec(memory_space=pltpu.HBM)] * 3,
        scratch_shapes=[
            pltpu.VMEM((docs, width), f32),
            pltpu.VMEM((2, 1, docs), i32),
            pltpu.SemaphoreType.DMA((3,)),
        ],
    )(*(in_hbm(x) for x in (embeddings, cluster.reshape(1, docs), order.reshape(1, docs))))
    chunks = packed.reshape(CLUSTERS, TILES, 2, LANES)

    def exchange(sent):
        return lax.all_to_all(sent, ("x", "zy"), split_axis=0, concat_axis=0, tiled=True)

    def keep(sent):
        return sent

    core = lax.axis_index("core")
    early = lax.cond(core == 1, exchange, keep, chunks)
    other = lax.ppermute(early, "core", [(1, 0)]).reshape(tiles)
    late = lax.cond(core == 0, exchange, keep, chunks).reshape(tiles)
    early = early.reshape(tiles)
    flops = 2 * slots * slots * width
    line = shape((8, slots), f32)
    queries, rank, first, away = call(
        first_kernel, (shape((width, slots), bf16), line, line, line), flops, 3 * moved
    )(early, late, other)
    away = lax.ppermute(away, "core", [(0, 1), (1, 0)])
    best = call(second_kernel, line, flops, 2 * moved)(late, queries, rank, first)
    best = call(merge_kernel, shape((CLUSTERS, LANES), f32), 0, CLUSTERS * LANES * 4)(best, away)
    back = lax.all_to_all(best, ("x", "zy"), split_axis=0, concat_axis=0, tiled=True)
    result = call(unpack_kernel, shape((1, docs), f32), 0, CLUSTERS * LANES * 4)(back, where)
    return result.reshape(docs)


def solution(mesh):
    devices = mesh.devices.reshape(-1, CORES, mesh.shape["narrow"])
    chips = Mesh(devices, ("zy", "core", "x"))
    axes = ("zy", "core", "x")
    return jax.shard_map(
        per_device,
        mesh=chips,
        in_specs=(P(axes, None), P(axes), P(axes)),
        out_specs=P(axes),
        check_vma=False,
    )
```

profile of v0, /device:TPU:0, one launch (start us, length us, event | category | flops | bytes accessed | tf_op | source)
XLA Modules:
  0.0 49.0 jit_solution(2027032350167248251)
XLA Ops:
  0.0 1.7 %shard_map.37 = (bf16[16,33,8,128]{3,2,1,0:T(8,128)(2,1)S(1)}, s32[8,128]{1,0:T(8,128)S(1)}) custom-call(f32[128,1024]{1,0:T(8,128)} %rows_hbm.1, s32[1,128]{1,0:T(1,128)} %bitcast.21, s32[1,128]{1,0:T(1,128)} %bitcast.22), custom_call_target="tpu_custom_call" | custom-call | flops 134217728 | bytes 1605632 | tf_op jit(solution)/shard_map/pallas_call | solution.py:206
  1.7 0.8 %conditional.3 = (bf16[64,33,2,128]{3,2,1,0:T(2,128)(2,1)S(1)}) conditional(s32[]{:T(128)} %convert_element_type.7, bf16[64,33,2,128]{3,2,1,0:T(2,128)(2,1)S(1)} %bitcast.14, bf16[64,33,2,128]{3,2,1,0:T(2,128)(2,1)S(1)} %bitcast.15), branch_computations={%region_2.0_spmd, %region_3.0_spmd} | conditional | bytes 2162696 | solution.py:227
  1.7 0.7 %copy.7 = bf16[64,33,2,128]{3,2,1,0:T(2,128)(2,1)S(1)} copy(bf16[64,33,2,128]{3,2,1,0:T(2,128)(2,1)S(1)} %param.2) | data formatting | bytes 2162688 | tf_op jit(solution)/shard_map/cond
  2.4 1.3 %collective-permute-start = (bf16[64,33,2,128]{3,2,1,0:T(2,128)(2,1)S(1)}, bf16[64,33,2,128]{3,2,1,0:T(2,128)(2,1)S(1)}, u32[]{:S(2)}, u32[]{:S(2)}) collective-permute-start(bf16[64,33,2,128]{3,2,1,0:T(2,128)(2,1)S(1)} %get-tuple-element.43), channel_id=1, source_target_pairs={{4,0},{5,1},{6,2},{7,3},{12,8},{13,9},{14,10},{15,11},{20,16},{21,... | collective-permute-start | bytes 3244040 | tf_op jit(solution)/shard_map/ppermute | solution.py:228
  3.8 28.1 %conditional.2 = (bf16[64,33,2,128]{3,2,1,0:T(2,128)(2,1)S(1)}) conditional(s32[]{:T(128)} %convert_element_type.6, bf16[64,33,2,128]{3,2,1,0:T(2,128)(2,1)S(1)} %bitcast.16, bf16[64,33,2,128]{3,2,1,0:T(2,128)(2,1)S(1)} %bitcast.17), branch_computations={%region_0.0_spmd, %region_1.0_spmd} | conditional | bytes 4325384 | solution.py:229
  3.8 0.7 %copy.9 = bf16[64,33,2,128]{3,2,1,0:T(2,128)(2,1)S(1)} copy(bf16[64,33,2,128]{3,2,1,0:T(2,128)(2,1)S(1)} %param.1) | data formatting | bytes 2162688 | tf_op jit(solution)/shard_map/cond
  4.5 27.4 %all_to_all.19 = bf16[64,33,2,128]{3,2,1,0:T(2,128)(2,1)S(1)} all-to-all(bf16[64,33,2,128]{3,2,1,0:T(2,128)(2,1)S(1)} %copy.9), channel_id=1, replica_groups=mesh['zy'=16,'core'=2,'x'=4] {'x','zy'}, dimensions={0} | all-to-all | bytes 2162688 | tf_op jit(solution)/shard_map/cond/branch_1_fun/all_to_all | solution.py:221
  31.9 0.0 collective-permute-done
  31.9 1.0 %shard_map.38 = (bf16[1024,512]{1,0:T(8,128)(2,1)S(1)}, f32[8,512]{1,0:T(8,128)S(1)}, f32[8,512]{1,0:T(8,128)S(1)}, f32[8,512]{1,0:T(8,128)S(1)}) custom-call(bf16[16,33,8,128]{3,2,1,0:T(8,128)(2,1)S(1)} %bitcast.20, bf16[16,33,8,128]{3,2,1,0:T(8,128)(2,1)S(1)} %bitcast.18, bf16[16,33,8,128]{3,2,1,0:T(8,128)(2,1)S(1)} %bitcast.11), custom_call_target="tpu_custom_call" | custom-call | flops 536870912 | bytes 3244032 | tf_op jit(solution)/shard_map/pallas_call | solution.py:233
  32.8 0.1 collective-permute-start.1
  32.9 0.7 %shard_map.39.best_ref = f32[8,512]{1,0:T(8,128)S(1)} custom-call(bf16[16,33,8,128]{3,2,1,0:T(8,128)(2,1)S(1)} %bitcast.19, bf16[1024,512]{1,0:T(8,128)(2,1)S(1)} %get-tuple-element.34.queries_ref, f32[8,512]{1,0:T(8,128)S(1)} %get-tuple-element.35.rank_ref, f32[8,512]{1,0:T(8,128)S(1)} %get-tuple-element.36.first_ref), custom_call_target="tpu_custom_call" | custom-call | flops 536870912 | bytes 2162688 | tf_op jit(solution)/shard_map/pallas_call | solution.py:237
  33.7 0.4 collective-permute-done.1.away_ref
  34.1 14.2 %all_to_all.21 = f32[64,1,128]{2,1,0:T(1,128)S(1)} all-to-all(f32[64,1,128]{2,1,0:T(1,128)S(1)} %bitcast.13), channel_id=1, replica_groups=mesh['zy'=16,'core'=2,'x'=4] {'x','zy'}, dimensions={0} | all-to-all | bytes 65536 | tf_op jit(solution)/shard_map/all_to_all | solution.py:239
  48.3 0.7 %shard_map.41 = f32[1,128]{1,0:T(1,128)} custom-call(f32[64,128]{1,0:T(8,128)S(1)} %bitcast.12, s32[8,128]{1,0:T(8,128)S(1)} %get-tuple-element.38.where_ref), custom_call_target="tpu_custom_call" | custom-call | bytes 32768 | tf_op jit(solution)/shard_map/pallas_call | solution.py:240
  (1 shorter events, 0.0 us)
Async XLA Ops:
  2.4 29.4 %collective-permute-start = (bf16[64,33,2,128]{3,2,1,0:T(2,128)(2,1)S(1)}, bf16[64,33,2,128]{3,2,1,0:T(2,128)(2,1)S(1)}, u32[]{:S(2)}, u32[]{:S(2)}) collective-permute-start(bf16[64,33,2,128]{3,2,1,0:T(2,128)(2,1)S(1)} %get-tuple-element.43), channel_id=1, source_target_pairs={{4,0},{5,1},{6,2},{7,3},{12,8},{13,9},{14,10},{15,11},{20,16},{21,... | collective-permute-start | bytes 3244040 | tf_op jit(solution)/shard_map/ppermute | solution.py:228
  32.8 1.3 %collective-permute-start.1 = (f32[8,512]{1,0:T(8,128)S(1)}, f32[8,512]{1,0:T(8,128)S(1)}, u32[]{:S(2)}, u32[]{:S(2)}) collective-permute-start(f32[8,512]{1,0:T(8,128)S(1)} %get-tuple-element.37), channel_id=1, source_target_pairs={{0,4},{4,0},{1,5},{5,1},{2,6},{6,2},{3,7},{7,3},{8,12},{12,8},{9,1... | collective-permute-start | bytes 49160 | tf_op jit(solution)/shard_map/ppermute | solution.py:236
where the time goes:
time: 49.2 us; the launch traced here: 49 us
  blocking collectives  41.6 us (85%)
  Pallas kernels  4.05 us (8%)
  local copies, waits for them, and re-layouts  1.49 us (3%)
  starting transfers between devices  1.38 us (3%)
    all_to_all x1, blocking collectives, exchange(): lax.all_to_all(sent, ('x', 'zy'), split_axis=0, concat_axis=0, tiled=True)  27.4 us
    all_to_all x1, blocking collectives, per_device(): lax.all_to_all(best, ('x', 'zy'), split_axis=0, concat_axis=0, tiled=True)  14.2 us
    pallas_call x1, Pallas kernels, per_device(): call(pack_kernel, (shape(tiles, bf16), shape((8, docs), i32)), 2 * slots...  1.66 us
    cond x2, local copies, waits for them, and re-layouts  1.49 us
    ppermute x1, starting transfers between devices, per_device(): other = lax.ppermute(early, 'core', [(1, 0)]).reshape(tiles)  1.29 us
  transfers between devices with their start and end apart: 2, of which 1 were waited for; matrix products, arithmetic and copies ran while one was open for 2% of the time, Pallas kernels for 1%

commit v1 on v0

--- a/solution.py
+++ b/solution.py
@@ -14,6 +14,7 @@
 GROUPS = CLUSTERS // CHUNKS
 PART = GROUPS * SLOTS
 TILES = 33
+MARKS = 16
 epsilon = 1e-06
 
 VMEM = 32 * 1024 * 1024
@@ -112,52 +113,70 @@
     step = 2 * LANES
     for at in range(0, queries_ref.shape[1], step):
         similar = jnp.dot(
-            keys, queries_ref[:, at : at + step], preferred_element_type=jnp.float32
+            keys, queries_ref[: keys.shape[1], at : at + step], preferred_element_type=jnp.float32
         )
         for lane in range(0, step, LANES):
             yield at + lane, similar[:, lane : lane + LANES]
 
 
-def maxima(keys, key_rank, queries_ref, rank_ref):
+def maxima(keys, key_rank, queries_ref, query_rank):
     for at, similar in similarities(keys, queries_ref):
-        allowed = key_rank < rank_ref[0:1, at : at + LANES]
+        allowed = key_rank < query_rank[0:1, at : at + LANES]
         yield at, largest(jnp.where(allowed, similar, -1.0))
 
 
-def first_kernel(early_ref, late_ref, other_ref, queries_ref, rank_ref, best_ref, away_ref):
-    core = lax.axis_index("core")
-
-    def turn(rows, ranks):
+def turn_kernel(early_ref, turned_ref, best_ref):
+    core = lax.axis_index("core")
+    width = turned_ref.shape[0] - MARKS
+
+    @pl.when(core == 0)
+    def _():
+        best_ref[...] = jnp.full(best_ref.shape, -1.0, jnp.float32)
+
+    @pl.when(core != 0)
+    def _():
+        rows, ranks = unfold(early_ref)
+        turned_ref[:width] = rows.T
+        rank = ranks.T[0:MARKS]
+        high = jnp.floor(rank * 0.0625)
+        parts = jnp.where(iota(rank.shape, 0) == 0, high, rank - high * 16.0)
+        turned_ref[width:] = parts.astype(jnp.bfloat16)
+        for at, best in maxima(rows, ranks, turned_ref, rank):
+            best_ref[:, at : at + LANES] = best
+
+
+def first_kernel(late_ref, other_ref, cross_ref, away_ref):
+    core = lax.axis_index("core")
+    width = other_ref.shape[0] - MARKS
+
+    @pl.when(core == 0)
+    def _():
+        rows, ranks = unfold(late_ref)
+        marks = other_ref[width:].astype(jnp.float32)
+        other_rank = marks[0:1] * 16.0 + marks[1:2]
+        best = jnp.full(ranks.shape, -1.0, jnp.float32)
+        for at, similar in similarities(rows, other_ref):
+            rank = other_rank[:, at : at + LANES]
+            away_ref[:, at : at + LANES] = largest(jnp.where(ranks < rank, similar, -1.0))
+            best = jnp.maximum(best, jnp.where(rank < ranks, similar, -1.0))
+        cross_ref[...] = best
+
+    @pl.when(core != 0)
+    def _():
+        away_ref[...] = jnp.full(away_ref.shape, -1.0, jnp.float32)
+        cross_ref[...] = jnp.full(cross_ref.shape, -1.0, jnp.float32)
+
+
+def second_kernel(late_ref, first_ref, cross_ref, best_ref, queries_ref):
+    core = lax.axis_index("core")
+
+    @pl.when(core == 0)
+    def _():
+        rows, ranks = unfold(late_ref)
         queries_ref[...] = rows.T
-        rank_ref[...] = ranks.T[0:8]
-
-    @pl.when(core == 0)
-    def _():
-        turn(*unfold(late_ref))
-        keys, key_rank = unfold(other_ref)
-        away = jnp.full(key_rank.shape, -1.0, jnp.float32)
-        for at, similar in similarities(keys, queries_ref):
-            rank = rank_ref[0:1, at : at + LANES]
-            best_ref[:, at : at + LANES] = largest(jnp.where(key_rank < rank, similar, -1.0))
-            away = jnp.maximum(away, jnp.where(rank < key_rank, similar, -1.0))
-        away_ref[...] = largest(away.T)
-
-    @pl.when(core != 0)
-    def _():
-        rows, ranks = unfold(early_ref)
-        turn(rows, ranks)
-        for at, best in maxima(rows, ranks, queries_ref, rank_ref):
-            best_ref[:, at : at + LANES] = best
-        away_ref[...] = jnp.full(away_ref.shape, -1.0, jnp.float32)
-
-
-def second_kernel(late_ref, queries_ref, rank_ref, first_ref, best_ref):
-    core = lax.axis_index("core")
-
-    @pl.when(core == 0)
-    def _():
-        for at, best in maxima(*unfold(late_ref), queries_ref, rank_ref):
-            best_ref[:, at : at + LANES] = jnp.maximum(best, first_ref[:, at : at + LANES])
+        cross = largest(cross_ref[...].T)
+        for at, best in maxima(rows, ranks, queries_ref, ranks.T[0:8]):
+            best_ref[:, at : at + LANES] = jnp.maximum(best, cross[:, at : at + LANES])
 
     @pl.when(core != 0)
     def _():
@@ -225,16 +244,27 @@
 
     core = lax.axis_index("core")
     early = lax.cond(core == 1, exchange, keep, chunks)
-    other = lax.ppermute(early, "core", [(1, 0)]).reshape(tiles)
     late = lax.cond(core == 0, exchange, keep, chunks).reshape(tiles)
-    early = early.reshape(tiles)
     flops = 2 * slots * slots * width
     line = shape((8, slots), f32)
-    queries, rank, first, away = call(
-        first_kernel, (shape((width, slots), bf16), line, line, line), flops, 3 * moved
-    )(early, late, other)
+    turned, first = call(
+        turn_kernel,
+        (pltpu.VMEM((width + MARKS, slots), bf16), pltpu.VMEM((8, slots), f32)),
+        flops,
+        2 * moved,
+    )(pltpu.with_memory_space_constraint(early.reshape(tiles), pltpu.VMEM))
+    other = lax.ppermute(turned, "core", [(1, 0)])
+    cross, away = call(first_kernel, (shape((slots, LANES), f32), line), flops, 2 * moved)(
+        late, other
+    )
     away = lax.ppermute(away, "core", [(0, 1), (1, 0)])
-    best = call(second_kernel, line, flops, 2 * moved)(late, queries, rank, first)
+    best = call(
+        second_kernel,
+        line,
+        flops,
+        2 * moved,
+        scratch_shapes=[pltpu.VMEM((width, slots), bf16)],
+    )(late, first, cross)
     best = call(merge_kernel, shape((CLUSTERS, LANES), f32), 0, CLUSTERS * LANES * 4)(best, away)
     back = lax.all_to_all(best, ("x", "zy"), split_axis=0, concat_axis=0, tiled=True)
     result = call(unpack_kernel, shape((1, docs), f32), 0, CLUSTERS * LANES * 4)(back, where)

time: 49.2 us -> 49.1 us (level)
    pallas_call x2 -> x3, Pallas kernels: 1.69 us -> 1.64 us  [the longest x1 0.83 us: per_device(): call(second_kernel, line, flops, 2 * moved, scratch_shapes=[pltpu.VMEM((w...]
  transfers between devices with their start and end apart: 2 -> 2, of which waited for: 1 -> 1; matrix products, arithmetic and copies ran while one was open for 2% -> 2% of each run, Pallas kernels for 1% -> 2%
where the time goes in v1:
time: 49.1 us; the launch traced here: 48.9 us
  blocking collectives  41.6 us (85%)
  Pallas kernels  4 us (8%)
  local copies, waits for them, and re-layouts  1.49 us (3%)
  starting transfers between devices  1.38 us (3%)
    all_to_all x1, blocking collectives, exchange(): lax.all_to_all(sent, ('x', 'zy'), split_axis=0, concat_axis=0, tiled=True)  27.3 us
    all_to_all x1, blocking collectives, per_device(): lax.all_to_all(best, ('x', 'zy'), split_axis=0, concat_axis=0, tiled=True)  14.3 us
    pallas_call x1, Pallas kernels, per_device(): call(pack_kernel, (shape(tiles, bf16), shape((8, docs), i32)), 2 * slots...  1.66 us
    cond x2, local copies, waits for them, and re-layouts  1.49 us
    ppermute x1, starting transfers between devices, per_device(): other = lax.ppermute(turned, 'core', [(1, 0)])  1.29 us
  transfers between devices with their start and end apart: 2, of which 1 were waited for; matrix products, arithmetic and copies ran while one was open for 2% of the time, Pallas kernels for 2%

profile of v1, /device:TPU:0, one launch (start us, length us, event | category | flops | bytes accessed | tf_op | source)
XLA Modules:
  0.0 48.9 jit_solution(16302174479713710299)
XLA Ops:
  0.0 1.7 %shard_map.37 = (bf16[16,33,8,128]{3,2,1,0:T(8,128)(2,1)S(1)}, s32[8,128]{1,0:T(8,128)S(1)}) custom-call(f32[128,1024]{1,0:T(8,128)} %rows_hbm.1, s32[1,128]{1,0:T(1,128)} %bitcast.19, s32[1,128]{1,0:T(1,128)} %bitcast.20), custom_call_target="tpu_custom_call" | custom-call | flops 134217728 | bytes 1605632 | tf_op jit(solution)/shard_map/pallas_call | solution.py:225
  1.7 0.8 %conditional.3 = (bf16[64,33,2,128]{3,2,1,0:T(2,128)(2,1)S(1)}) conditional(s32[]{:T(128)} %convert_element_type.7, bf16[64,33,2,128]{3,2,1,0:T(2,128)(2,1)S(1)} %bitcast.13, bf16[64,33,2,128]{3,2,1,0:T(2,128)(2,1)S(1)} %bitcast.14), branch_computations={%region_2.0_spmd, %region_3.0_spmd} | conditional | bytes 2162696 | solution.py:246
  1.7 0.7 %copy.7 = bf16[64,33,2,128]{3,2,1,0:T(2,128)(2,1)S(1)} copy(bf16[64,33,2,128]{3,2,1,0:T(2,128)(2,1)S(1)} %param.2) | data formatting | bytes 2162688 | tf_op jit(solution)/shard_map/cond
  2.5 1.3 %collective-permute-start = (bf16[1040,512]{1,0:T(8,128)(2,1)S(1)}, bf16[1040,512]{1,0:T(8,128)(2,1)S(1)}, u32[]{:S(2)}, u32[]{:S(2)}) collective-permute-start(bf16[1040,512]{1,0:T(8,128)(2,1)S(1)} %get-tuple-element.29), channel_id=1, source_target_pairs={{4,0},{5,1},{6,2},{7,3},{12,8},{13,9},{14,10},{15,11},{20,16},{21,... | collective-permute-start | bytes 3194888 | tf_op jit(solution)/shard_map/ppermute | solution.py:256
  3.8 28.1 %conditional.2 = (bf16[64,33,2,128]{3,2,1,0:T(2,128)(2,1)S(1)}) conditional(s32[]{:T(128)} %convert_element_type.6, bf16[64,33,2,128]{3,2,1,0:T(2,128)(2,1)S(1)} %bitcast.15, bf16[64,33,2,128]{3,2,1,0:T(2,128)(2,1)S(1)} %bitcast.16), branch_computations={%region_0.0_spmd, %region_1.0_spmd} | conditional | bytes 4325384 | solution.py:247
  3.8 0.7 %copy.9 = bf16[64,33,2,128]{3,2,1,0:T(2,128)(2,1)S(1)} copy(bf16[64,33,2,128]{3,2,1,0:T(2,128)(2,1)S(1)} %param.1) | data formatting | bytes 2162688 | tf_op jit(solution)/shard_map/cond
  4.5 27.3 %all_to_all.19 = bf16[64,33,2,128]{3,2,1,0:T(2,128)(2,1)S(1)} all-to-all(bf16[64,33,2,128]{3,2,1,0:T(2,128)(2,1)S(1)} %copy.9), channel_id=1, replica_groups=mesh['zy'=16,'core'=2,'x'=4] {'x','zy'}, dimensions={0} | all-to-all | bytes 2162688 | tf_op jit(solution)/shard_map/cond/branch_1_fun/all_to_all | solution.py:240
  31.9 0.0 collective-permute-done.other_ref
  31.9 0.8 %shard_map.39 = (f32[512,128]{1,0:T(8,128)S(1)}, f32[8,512]{1,0:T(8,128)S(1)}) custom-call(bf16[16,33,8,128]{3,2,1,0:T(8,128)(2,1)S(1)} %bitcast.17, bf16[1040,512]{1,0:T(8,128)(2,1)S(1)} %collective-permute-done.other_ref), custom_call_target="tpu_custom_call" | custom-call | flops 536870912 | bytes 2162688 | tf_op jit(solution)/shard_map/pallas_call | solution.py:257
  32.7 0.1 collective-permute-start.1
  32.8 0.8 %shard_map.40.best_ref = f32[8,512]{1,0:T(8,128)S(1)} custom-call(bf16[16,33,8,128]{3,2,1,0:T(8,128)(2,1)S(1)} %bitcast.18, f32[8,512]{1,0:T(8,128)S(1)} %get-tuple-element.28.first_ref, f32[512,128]{1,0:T(8,128)S(1)} %get-tuple-element.30.cross_ref), custom_call_target="tpu_custom_call" | custom-call | flops 536870912 | bytes 2162688 | tf_op jit(solution)/shard_map/pallas_call | solution.py:261
  33.6 0.3 collective-permute-done.1.away_ref
  33.9 14.3 %all_to_all.21 = f32[64,1,128]{2,1,0:T(1,128)S(1)} all-to-all(f32[64,1,128]{2,1,0:T(1,128)S(1)} %bitcast.12), channel_id=1, replica_groups=mesh['zy'=16,'core'=2,'x'=4] {'x','zy'}, dimensions={0} | all-to-all | bytes 65536 | tf_op jit(solution)/shard_map/all_to_all | solution.py:269
  48.2 0.7 %shard_map.42 = f32[1,128]{1,0:T(1,128)} custom-call(f32[64,128]{1,0:T(8,128)S(1)} %bitcast.11, s32[8,128]{1,0:T(8,128)S(1)} %get-tuple-element.32.where_ref), custom_call_target="tpu_custom_call" | custom-call | bytes 32768 | tf_op jit(solution)/shard_map/pallas_call | solution.py:270
  (2 shorter events, 0.0 us)
Async XLA Ops:
  2.5 29.4 %collective-permute-start = (bf16[1040,512]{1,0:T(8,128)(2,1)S(1)}, bf16[1040,512]{1,0:T(8,128)(2,1)S(1)}, u32[]{:S(2)}, u32[]{:S(2)}) collective-permute-start(bf16[1040,512]{1,0:T(8,128)(2,1)S(1)} %get-tuple-element.29), channel_id=1, source_target_pairs={{4,0},{5,1},{6,2},{7,3},{12,8},{13,9},{14,10},{15,11},{20,16},{21,... | collective-permute-start | bytes 3194888 | tf_op jit(solution)/shard_map/ppermute | solution.py:256
  32.7 1.3 %collective-permute-start.1 = (f32[8,512]{1,0:T(8,128)S(1)}, f32[8,512]{1,0:T(8,128)S(1)}, u32[]{:S(2)}, u32[]{:S(2)}) collective-permute-start(f32[8,512]{1,0:T(8,128)S(1)} %get-tuple-element.31), channel_id=1, source_target_pairs={{0,4},{4,0},{1,5},{5,1},{2,6},{6,2},{3,7},{7,3},{8,12},{12,8},{9,1... | collective-permute-start | bytes 49160 | tf_op jit(solution)/shard_map/ppermute | solution.py:260

commit v2 on v1

--- a/solution.py
+++ b/solution.py
@@ -167,29 +167,28 @@
         cross_ref[...] = jnp.full(cross_ref.shape, -1.0, jnp.float32)
 
 
-def second_kernel(late_ref, first_ref, cross_ref, best_ref, queries_ref):
-    core = lax.axis_index("core")
-
-    @pl.when(core == 0)
+def lines_of(best_ref, best):
+    best = jnp.max(best, axis=0, keepdims=True)
+    lines = [best[:, at : at + LANES] for at in range(0, best.shape[1], LANES)]
+    lines = jnp.concatenate(lines + lines)
+    for at in range(0, CLUSTERS, 8):
+        best_ref[at : at + 8] = lines
+
+
+def second_kernel(late_ref, cross_ref, out_ref, queries_ref):
+    @pl.when(lax.axis_index("core") == 0)
     def _():
         rows, ranks = unfold(late_ref)
         queries_ref[...] = rows.T
         cross = largest(cross_ref[...].T)
-        for at, best in maxima(rows, ranks, queries_ref, ranks.T[0:8]):
-            best_ref[:, at : at + LANES] = jnp.maximum(best, cross[:, at : at + LANES])
-
-    @pl.when(core != 0)
-    def _():
-        best_ref[...] = first_ref[...]
-
-
-def merge_kernel(best_ref, away_ref, out_ref):
-    away = jnp.where(lax.axis_index("core") == 0, -1.0, away_ref[...])
-    best = jnp.max(jnp.maximum(best_ref[...], away), axis=0, keepdims=True)
-    lines = [best[:, at : at + LANES] for at in range(0, best.shape[1], LANES)]
-    lines = jnp.concatenate(lines + lines)
-    for at in range(0, CLUSTERS, 8):
-        out_ref[at : at + 8] = lines
+        best = [x for _, x in maxima(rows, ranks, queries_ref, ranks.T[0:8])]
+        lines_of(out_ref, jnp.maximum(jnp.concatenate(best, axis=1), cross))
+
+
+def merge_kernel(first_ref, away_ref, out_ref):
+    @pl.when(lax.axis_index("core") != 0)
+    def _():
+        lines_of(out_ref, jnp.maximum(first_ref[...], away_ref[...]))
 
 
 def unpack_kernel(best_ref, where_ref, out_ref):
@@ -258,15 +257,17 @@
         late, other
     )
     away = lax.ppermute(away, "core", [(0, 1), (1, 0)])
+    answer = shape((CLUSTERS, LANES), f32)
     best = call(
         second_kernel,
-        line,
+        answer,
         flops,
         2 * moved,
         scratch_shapes=[pltpu.VMEM((width, slots), bf16)],
-    )(late, first, cross)
-    best = call(merge_kernel, shape((CLUSTERS, LANES), f32), 0, CLUSTERS * LANES * 4)(best, away)
-    back = lax.all_to_all(best, ("x", "zy"), split_axis=0, concat_axis=0, tiled=True)
+    )(late, cross)
+    back = lax.cond(core == 0, exchange, keep, best)
+    best = call(merge_kernel, answer, 0, CLUSTERS * LANES * 4)(first, away)
+    back = lax.cond(core == 1, lambda sent, kept: exchange(sent), lambda sent, kept: kept, best, back)
     result = call(unpack_kernel, shape((1, docs), f32), 0, CLUSTERS * LANES * 4)(back, where)
     return result.reshape(docs)
 

time: 49.1 us -> 48.8 us (level)
    all_to_all x1 -> x0, blocking collectives: 14.3 us -> none  [per_device(): lax.all_to_all(best, ('x', 'zy'), split_axis=0, concat_axis=0, tiled=True)]
    all_to_all x1 -> x2, blocking collectives: 27.3 us -> 41.6 us  [exchange(): lax.all_to_all(sent, ('x', 'zy'), split_axis=0, concat_axis=0, tiled=True)]
    cond x2 -> x3, local copies, waits for them, and re-layouts: 1.49 us -> 1.49 us
  transfers between devices with their start and end apart: 2 -> 2, of which waited for: 1 -> 0; matrix products, arithmetic and copies ran while one was open for 2% -> 2% of each run, Pallas kernels for 2% -> 2%
where the time goes in v2:
time: 48.8 us; the launch traced here: 48.6 us
  blocking collectives  41.6 us (85%)
  Pallas kernels  4 us (8%)
  local copies, waits for them, and re-layouts  1.49 us (3%)
  starting transfers between devices  1.38 us (3%)
    all_to_all x2, blocking collectives, exchange(): lax.all_to_all(sent, ('x', 'zy'), split_axis=0, concat_axis=0, tiled=True)  41.6 us
    pallas_call x1, Pallas kernels, per_device(): call(pack_kernel, (shape(tiles, bf16), shape((8, docs), i32)), 2 * slots...  1.66 us
    cond x3, local copies, waits for them, and re-layouts  1.49 us
    ppermute x1, starting transfers between devices, per_device(): other = lax.ppermute(turned, 'core', [(1, 0)])  1.29 us
  transfers between devices with their start and end apart: 2, of which 0 were waited for; matrix products, arithmetic and copies ran while one was open for 2% of the time, Pallas kernels for 2%

profile of v2, /device:TPU:0, one launch (start us, length us, event | category | flops | bytes accessed | tf_op | source)
XLA Modules:
  0.0 48.6 jit_solution(5522831650945210583)
XLA Ops:
  0.0 1.7 %shard_map.37 = (bf16[16,33,8,128]{3,2,1,0:T(8,128)(2,1)S(1)}, s32[8,128]{1,0:T(8,128)S(1)}) custom-call(f32[128,1024]{1,0:T(8,128)} %rows_hbm.1, s32[1,128]{1,0:T(1,128)} %bitcast.21, s32[1,128]{1,0:T(1,128)} %bitcast.22), custom_call_target="tpu_custom_call" | custom-call | flops 134217728 | bytes 1605632 | tf_op jit(solution)/shard_map/pallas_call | solution.py:224
  1.7 0.8 %conditional.5 = (bf16[64,33,2,128]{3,2,1,0:T(2,128)(2,1)S(1)}) conditional(s32[]{:T(128)} %convert_element_type.8, bf16[64,33,2,128]{3,2,1,0:T(2,128)(2,1)S(1)} %bitcast.11, bf16[64,33,2,128]{3,2,1,0:T(2,128)(2,1)S(1)} %bitcast.12), branch_computations={%region_2.0_spmd, %region_3.0_spmd} | conditional | bytes 2162696 | solution.py:245
  1.7 0.7 %copy.6 = bf16[64,33,2,128]{3,2,1,0:T(2,128)(2,1)S(1)} copy(bf16[64,33,2,128]{3,2,1,0:T(2,128)(2,1)S(1)} %param.2) | data formatting | bytes 2162688 | tf_op jit(solution)/shard_map/cond
  2.5 1.3 %collective-permute-start = (bf16[1040,512]{1,0:T(8,128)(2,1)S(1)}, bf16[1040,512]{1,0:T(8,128)(2,1)S(1)}, u32[]{:S(2)}, u32[]{:S(2)}) collective-permute-start(bf16[1040,512]{1,0:T(8,128)(2,1)S(1)} %get-tuple-element.38), channel_id=1, source_target_pairs={{4,0},{5,1},{6,2},{7,3},{12,8},{13,9},{14,10},{15,11},{20,16},{21,... | collective-permute-start | bytes 3194888 | tf_op jit(solution)/shard_map/ppermute | solution.py:255
  3.8 28.1 %conditional.4 = (bf16[64,33,2,128]{3,2,1,0:T(2,128)(2,1)S(1)}) conditional(s32[]{:T(128)} %convert_element_type.9, bf16[64,33,2,128]{3,2,1,0:T(2,128)(2,1)S(1)} %bitcast.13, bf16[64,33,2,128]{3,2,1,0:T(2,128)(2,1)S(1)} %bitcast.14), branch_computations={%region_0.0_spmd, %region_1.0_spmd} | conditional | bytes 4325384 | solution.py:246
  3.8 0.7 %copy.12 = bf16[64,33,2,128]{3,2,1,0:T(2,128)(2,1)S(1)} copy(bf16[64,33,2,128]{3,2,1,0:T(2,128)(2,1)S(1)} %param.1) | data formatting | bytes 2162688 | tf_op jit(solution)/shard_map/cond
  4.5 27.3 %all_to_all.26 = bf16[64,33,2,128]{3,2,1,0:T(2,128)(2,1)S(1)} all-to-all(bf16[64,33,2,128]{3,2,1,0:T(2,128)(2,1)S(1)} %copy.12), channel_id=1, replica_groups=mesh['zy'=16,'core'=2,'x'=4] {'x','zy'}, dimensions={0} | all-to-all | bytes 2162688 | tf_op jit(solution)/shard_map/cond/branch_1_fun/all_to_all | solution.py:239
  31.9 0.0 collective-permute-done.other_ref
  31.9 0.8 %shard_map.39 = (f32[512,128]{1,0:T(8,128)S(1)}, f32[8,512]{1,0:T(8,128)S(1)}) custom-call(bf16[16,33,8,128]{3,2,1,0:T(8,128)(2,1)S(1)} %bitcast.15, bf16[1040,512]{1,0:T(8,128)(2,1)S(1)} %collective-permute-done.other_ref), custom_call_target="tpu_custom_call" | custom-call | flops 536870912 | bytes 2162688 | tf_op jit(solution)/shard_map/pallas_call | solution.py:256
  32.7 0.1 collective-permute-start.1
  32.8 0.8 %shard_map.40 = f32[64,128]{1,0:T(8,128)S(1)} custom-call(bf16[16,33,8,128]{3,2,1,0:T(8,128)(2,1)S(1)} %bitcast.16, f32[512,128]{1,0:T(8,128)S(1)} %get-tuple-element.39.cross_ref), custom_call_target="tpu_custom_call" | custom-call | flops 536870912 | bytes 2162688 | tf_op jit(solution)/shard_map/pallas_call | solution.py:261
  33.6 14.3 %conditional.6 = (f32[64,128]{1,0:T(8,128)S(1)}) conditional(s32[]{:T(128)} %convert_element_type.9, f32[64,128]{1,0:T(8,128)S(1)} %shard_map.40, f32[64,128]{1,0:T(8,128)S(1)} %shard_map.40), branch_computations={%region_4.0_spmd, %region_5.0_spmd} | conditional | bytes 131080 | solution.py:268
  33.6 14.3 %all_to_all.28 = f32[64,1,128]{2,1,0:T(1,128)S(1)} all-to-all(f32[64,1,128]{2,1,0:T(1,128)S(1)} %copy.13), channel_id=1, replica_groups=mesh['zy'=16,'core'=2,'x'=4] {'x','zy'}, dimensions={0} | all-to-all | bytes 65536 | tf_op jit(solution)/shard_map/cond/branch_1_fun/all_to_all | solution.py:239
  47.9 0.0 collective-permute-done.1.away_ref
  47.9 0.7 %shard_map.42 = f32[1,128]{1,0:T(1,128)} custom-call(f32[64,128]{1,0:T(8,128)S(1)} %get-tuple-element.49.best_ref, s32[8,128]{1,0:T(8,128)S(1)} %get-tuple-element.42.where_ref), custom_call_target="tpu_custom_call" | custom-call | bytes 32768 | tf_op jit(solution)/shard_map/pallas_call | solution.py:271
  (4 shorter events, 0.0 us)
Async XLA Ops:
  2.5 29.4 %collective-permute-start = (bf16[1040,512]{1,0:T(8,128)(2,1)S(1)}, bf16[1040,512]{1,0:T(8,128)(2,1)S(1)}, u32[]{:S(2)}, u32[]{:S(2)}) collective-permute-start(bf16[1040,512]{1,0:T(8,128)(2,1)S(1)} %get-tuple-element.38), channel_id=1, source_target_pairs={{4,0},{5,1},{6,2},{7,3},{12,8},{13,9},{14,10},{15,11},{20,16},{21,... | collective-permute-start | bytes 3194888 | tf_op jit(solution)/shard_map/ppermute | solution.py:255
  32.7 15.3 %collective-permute-start.1 = (f32[8,512]{1,0:T(8,128)S(1)}, f32[8,512]{1,0:T(8,128)S(1)}, u32[]{:S(2)}, u32[]{:S(2)}) collective-permute-start(f32[8,512]{1,0:T(8,128)S(1)} %get-tuple-element.41), channel_id=1, source_target_pairs={{0,4},{4,0},{1,5},{5,1},{2,6},{6,2},{3,7},{7,3},{8,12},{12,8},{9,1... | collective-permute-start | bytes 49160 | tf_op jit(solution)/shard_map/ppermute | solution.py:259

commit v3 on v2

--- a/solution.py
+++ b/solution.py
@@ -175,13 +175,21 @@
         best_ref[at : at + 8] = lines
 
 
-def second_kernel(late_ref, cross_ref, out_ref, queries_ref):
+def second_kernel(late_ref, cross_ref, out_ref):
     @pl.when(lax.axis_index("core") == 0)
     def _():
         rows, ranks = unfold(late_ref)
-        queries_ref[...] = rows.T
         cross = largest(cross_ref[...].T)
-        best = [x for _, x in maxima(rows, ranks, queries_ref, ranks.T[0:8])]
+        line = ranks.T[0:1]
+        best = []
+        step = 2 * LANES
+        for at in range(0, rows.shape[0], step):
+            similar = lax.dot_general(
+                rows, rows[at : at + step], NT, preferred_element_type=jnp.float32
+            )
+            for lane in range(0, step, LANES):
+                allowed = ranks < line[:, at + lane : at + lane + LANES]
+                best.append(largest(jnp.where(allowed, similar[:, lane : lane + LANES], -1.0)))
         lines_of(out_ref, jnp.maximum(jnp.concatenate(best, axis=1), cross))
 
 
@@ -263,7 +271,6 @@
         answer,
         flops,
         2 * moved,
-        scratch_shapes=[pltpu.VMEM((width, slots), bf16)],
     )(late, cross)
     back = lax.cond(core == 0, exchange, keep, best)
     best = call(merge_kernel, answer, 0, CLUSTERS * LANES * 4)(first, away)

time: 48.8 us -> 48.8 us (level)
  no operation moved by 1% of the time
where the time goes in v3:
time: 48.8 us; the launch traced here: 48.6 us
  blocking collectives  41.6 us (85%)
  Pallas kernels  3.93 us (8%)
  local copies, waits for them, and re-layouts  1.49 us (3%)
  starting transfers between devices  1.38 us (3%)
    all_to_all x2, blocking collectives, exchange(): lax.all_to_all(sent, ('x', 'zy'), split_axis=0, concat_axis=0, tiled=True)  41.6 us
    pallas_call x1, Pallas kernels, per_device(): call(pack_kernel, (shape(tiles, bf16), shape((8, docs), i32)), 2 * slots...  1.66 us
    cond x3, local copies, waits for them, and re-layouts  1.49 us
    ppermute x1, starting transfers between devices, per_device(): other = lax.ppermute(turned, 'core', [(1, 0)])  1.29 us
  transfers between devices with their start and end apart: 2, of which 0 were waited for; matrix products, arithmetic and copies ran while one was open for 2% of the time, Pallas kernels for 2%

profile of v3, /device:TPU:0, one launch (start us, length us, event | category | flops | bytes accessed | tf_op | source)
XLA Modules:
  0.0 48.6 jit_solution(5805369976845553011)
XLA Ops:
  0.0 1.7 %shard_map.37 = (bf16[16,33,8,128]{3,2,1,0:T(8,128)(2,1)S(1)}, s32[8,128]{1,0:T(8,128)S(1)}) custom-call(f32[128,1024]{1,0:T(8,128)} %rows_hbm.1, s32[1,128]{1,0:T(1,128)} %bitcast.21, s32[1,128]{1,0:T(1,128)} %bitcast.22), custom_call_target="tpu_custom_call" | custom-call | flops 134217728 | bytes 1605632 | tf_op jit(solution)/shard_map/pallas_call | solution.py:232
  1.7 0.8 %conditional.5 = (bf16[64,33,2,128]{3,2,1,0:T(2,128)(2,1)S(1)}) conditional(s32[]{:T(128)} %convert_element_type.8, bf16[64,33,2,128]{3,2,1,0:T(2,128)(2,1)S(1)} %bitcast.11, bf16[64,33,2,128]{3,2,1,0:T(2,128)(2,1)S(1)} %bitcast.12), branch_computations={%region_2.0_spmd, %region_3.0_spmd} | conditional | bytes 2162696 | solution.py:253
  1.7 0.7 %copy.6 = bf16[64,33,2,128]{3,2,1,0:T(2,128)(2,1)S(1)} copy(bf16[64,33,2,128]{3,2,1,0:T(2,128)(2,1)S(1)} %param.2) | data formatting | bytes 2162688 | tf_op jit(solution)/shard_map/cond
  2.5 1.3 %collective-permute-start = (bf16[1040,512]{1,0:T(8,128)(2,1)S(1)}, bf16[1040,512]{1,0:T(8,128)(2,1)S(1)}, u32[]{:S(2)}, u32[]{:S(2)}) collective-permute-start(bf16[1040,512]{1,0:T(8,128)(2,1)S(1)} %get-tuple-element.38), channel_id=1, source_target_pairs={{4,0},{5,1},{6,2},{7,3},{12,8},{13,9},{14,10},{15,11},{20,16},{21,... | collective-permute-start | bytes 3194888 | tf_op jit(solution)/shard_map/ppermute | solution.py:263
  3.8 28.1 %conditional.4 = (bf16[64,33,2,128]{3,2,1,0:T(2,128)(2,1)S(1)}) conditional(s32[]{:T(128)} %convert_element_type.9, bf16[64,33,2,128]{3,2,1,0:T(2,128)(2,1)S(1)} %bitcast.13, bf16[64,33,2,128]{3,2,1,0:T(2,128)(2,1)S(1)} %bitcast.14), branch_computations={%region_0.0_spmd, %region_1.0_spmd} | conditional | bytes 4325384 | solution.py:254
  3.8 0.7 %copy.12 = bf16[64,33,2,128]{3,2,1,0:T(2,128)(2,1)S(1)} copy(bf16[64,33,2,128]{3,2,1,0:T(2,128)(2,1)S(1)} %param.1) | data formatting | bytes 2162688 | tf_op jit(solution)/shard_map/cond
  4.5 27.3 %all_to_all.26 = bf16[64,33,2,128]{3,2,1,0:T(2,128)(2,1)S(1)} all-to-all(bf16[64,33,2,128]{3,2,1,0:T(2,128)(2,1)S(1)} %copy.12), channel_id=1, replica_groups=mesh['zy'=16,'core'=2,'x'=4] {'x','zy'}, dimensions={0} | all-to-all | bytes 2162688 | tf_op jit(solution)/shard_map/cond/branch_1_fun/all_to_all | solution.py:247
  31.9 0.0 collective-permute-done.other_ref
  31.9 0.8 %shard_map.39 = (f32[512,128]{1,0:T(8,128)S(1)}, f32[8,512]{1,0:T(8,128)S(1)}) custom-call(bf16[16,33,8,128]{3,2,1,0:T(8,128)(2,1)S(1)} %bitcast.15, bf16[1040,512]{1,0:T(8,128)(2,1)S(1)} %collective-permute-done.other_ref), custom_call_target="tpu_custom_call" | custom-call | flops 536870912 | bytes 2162688 | tf_op jit(solution)/shard_map/pallas_call | solution.py:264
  32.7 0.1 collective-permute-start.1
  32.8 0.8 %shard_map.40 = f32[64,128]{1,0:T(8,128)S(1)} custom-call(bf16[16,33,8,128]{3,2,1,0:T(8,128)(2,1)S(1)} %bitcast.16, f32[512,128]{1,0:T(8,128)S(1)} %get-tuple-element.39.cross_ref), custom_call_target="tpu_custom_call" | custom-call | flops 536870912 | bytes 2162688 | tf_op jit(solution)/shard_map/pallas_call | solution.py:269
  33.5 14.3 %conditional.6 = (f32[64,128]{1,0:T(8,128)S(1)}) conditional(s32[]{:T(128)} %convert_element_type.9, f32[64,128]{1,0:T(8,128)S(1)} %shard_map.40, f32[64,128]{1,0:T(8,128)S(1)} %shard_map.40), branch_computations={%region_4.0_spmd, %region_5.0_spmd} | conditional | bytes 131080 | solution.py:275
  33.6 14.3 %all_to_all.28 = f32[64,1,128]{2,1,0:T(1,128)S(1)} all-to-all(f32[64,1,128]{2,1,0:T(1,128)S(1)} %copy.13), channel_id=1, replica_groups=mesh['zy'=16,'core'=2,'x'=4] {'x','zy'}, dimensions={0} | all-to-all | bytes 65536 | tf_op jit(solution)/shard_map/cond/branch_1_fun/all_to_all | solution.py:247
  47.9 0.0 collective-permute-done.1.away_ref
  47.9 0.7 %shard_map.42 = f32[1,128]{1,0:T(1,128)} custom-call(f32[64,128]{1,0:T(8,128)S(1)} %get-tuple-element.49.best_ref, s32[8,128]{1,0:T(8,128)S(1)} %get-tuple-element.42.where_ref), custom_call_target="tpu_custom_call" | custom-call | bytes 32768 | tf_op jit(solution)/shard_map/pallas_call | solution.py:278
  (4 shorter events, 0.0 us)
Async XLA Ops:
  2.5 29.4 %collective-permute-start = (bf16[1040,512]{1,0:T(8,128)(2,1)S(1)}, bf16[1040,512]{1,0:T(8,128)(2,1)S(1)}, u32[]{:S(2)}, u32[]{:S(2)}) collective-permute-start(bf16[1040,512]{1,0:T(8,128)(2,1)S(1)} %get-tuple-element.38), channel_id=1, source_target_pairs={{4,0},{5,1},{6,2},{7,3},{12,8},{13,9},{14,10},{15,11},{20,16},{21,... | collective-permute-start | bytes 3194888 | tf_op jit(solution)/shard_map/ppermute | solution.py:263
  32.7 15.2 %collective-permute-start.1 = (f32[8,512]{1,0:T(8,128)S(1)}, f32[8,512]{1,0:T(8,128)S(1)}, u32[]{:S(2)}, u32[]{:S(2)}) collective-permute-start(f32[8,512]{1,0:T(8,128)S(1)} %get-tuple-element.41), channel_id=1, source_target_pairs={{0,4},{4,0},{1,5},{5,1},{2,6},{6,2},{3,7},{7,3},{8,12},{12,8},{9,1... | collective-permute-start | bytes 49160 | tf_op jit(solution)/shard_map/ppermute | solution.py:267

commit v4 on v3

--- a/solution.py
+++ b/solution.py
@@ -19,6 +19,7 @@
 
 VMEM = 32 * 1024 * 1024
 NT = (((1,), (1,)), ((), ()))
+TN = (((0,), (0,)), ((), ()))
 
 
 def iota(shape, axis):
@@ -125,15 +126,10 @@
         yield at, largest(jnp.where(allowed, similar, -1.0))
 
 
-def turn_kernel(early_ref, turned_ref, best_ref):
-    core = lax.axis_index("core")
+def turn_kernel(early_ref, turned_ref):
     width = turned_ref.shape[0] - MARKS
 
-    @pl.when(core == 0)
-    def _():
-        best_ref[...] = jnp.full(best_ref.shape, -1.0, jnp.float32)
-
-    @pl.when(core != 0)
+    @pl.when(lax.axis_index("core") != 0)
     def _():
         rows, ranks = unfold(early_ref)
         turned_ref[:width] = rows.T
@@ -141,8 +137,6 @@
         high = jnp.floor(rank * 0.0625)
         parts = jnp.where(iota(rank.shape, 0) == 0, high, rank - high * 16.0)
         turned_ref[width:] = parts.astype(jnp.bfloat16)
-        for at, best in maxima(rows, ranks, turned_ref, rank):
-            best_ref[:, at : at + LANES] = best
 
 
 def first_kernel(late_ref, other_ref, cross_ref, away_ref):
@@ -175,7 +169,7 @@
         best_ref[at : at + 8] = lines
 
 
-def second_kernel(late_ref, cross_ref, out_ref):
+def second_kernel(late_ref, cross_ref, mine_ref, out_ref, first_ref):
     @pl.when(lax.axis_index("core") == 0)
     def _():
         rows, ranks = unfold(late_ref)
@@ -191,6 +185,25 @@
                 allowed = ranks < line[:, at + lane : at + lane + LANES]
                 best.append(largest(jnp.where(allowed, similar[:, lane : lane + LANES], -1.0)))
         lines_of(out_ref, jnp.maximum(jnp.concatenate(best, axis=1), cross))
+
+    @pl.when(lax.axis_index("core") != 0)
+    def _():
+        width = mine_ref.shape[0] - MARKS
+        marks = mine_ref[width:].astype(jnp.float32)
+        line = marks[0:1] * 16.0 + marks[1:2]
+        ranks = jnp.broadcast_to(line, (LANES, line.shape[1])).T
+        step = 2 * LANES
+        for at in range(0, line.shape[1], step):
+            similar = lax.dot_general(
+                mine_ref[:width],
+                mine_ref[:width, at : at + step],
+                TN,
+                preferred_element_type=jnp.float32,
+            )
+            for lane in range(0, step, LANES):
+                allowed = ranks < line[:, at + lane : at + lane + LANES]
+                best = largest(jnp.where(allowed, similar[:, lane : lane + LANES], -1.0))
+                first_ref[:, at + lane : at + lane + LANES] = best
 
 
 def merge_kernel(first_ref, away_ref, out_ref):
@@ -254,24 +267,17 @@
     late = lax.cond(core == 0, exchange, keep, chunks).reshape(tiles)
     flops = 2 * slots * slots * width
     line = shape((8, slots), f32)
-    turned, first = call(
-        turn_kernel,
-        (pltpu.VMEM((width + MARKS, slots), bf16), pltpu.VMEM((8, slots), f32)),
-        flops,
-        2 * moved,
-    )(pltpu.with_memory_space_constraint(early.reshape(tiles), pltpu.VMEM))
+    turned = call(turn_kernel, pltpu.VMEM((width + MARKS, slots), bf16), 0, 2 * moved)(
+        pltpu.with_memory_space_constraint(early.reshape(tiles), pltpu.VMEM)
+    )
     other = lax.ppermute(turned, "core", [(1, 0)])
     cross, away = call(first_kernel, (shape((slots, LANES), f32), line), flops, 2 * moved)(
         late, other
     )
     away = lax.ppermute(away, "core", [(0, 1), (1, 0)])
     answer = shape((CLUSTERS, LANES), f32)
-    best = call(
-        second_kernel,
-        answer,
-        flops,
-        2 * moved,
-    )(late, cross)
+    mine = pltpu.with_memory_space_constraint(turned, pltpu.VMEM)
+    best, first = call(second_kernel, (answer, line), flops, 2 * moved)(late, cross, mine)
     back = lax.cond(core == 0, exchange, keep, best)
     best = call(merge_kernel, answer, 0, CLUSTERS * LANES * 4)(first, away)
     back = lax.cond(core == 1, lambda sent, kept: exchange(sent), lambda sent, kept: kept, best, back)

time: 48.8 us -> 48.7 us (level)
  no operation moved by 1% of the time
where the time goes in v4:
time: 48.7 us; the launch traced here: 48.5 us
  blocking collectives  41.5 us (85%)
  Pallas kernels  3.93 us (8%)
  local copies, waits for them, and re-layouts  1.49 us (3%)
  starting transfers between devices  1.38 us (3%)
    all_to_all x2, blocking collectives, exchange(): lax.all_to_all(sent, ('x', 'zy'), split_axis=0, concat_axis=0, tiled=True)  41.5 us
    pallas_call x1, Pallas kernels, per_device(): call(pack_kernel, (shape(tiles, bf16), shape((8, docs), i32)), 2 * slots...  1.66 us
    cond x3, local copies, waits for them, and re-layouts  1.49 us
    ppermute x1, starting transfers between devices, per_device(): other = lax.ppermute(turned, 'core', [(1, 0)])  1.29 us
  transfers between devices with their start and end apart: 2, of which 0 were waited for; matrix products, arithmetic and copies ran while one was open for 2% of the time, Pallas kernels for 2%

profile of v4, /device:TPU:0, one launch (start us, length us, event | category | flops | bytes accessed | tf_op | source)
XLA Modules:
  0.0 48.5 jit_solution(16377101129674825254)
XLA Ops:
  0.0 1.7 %shard_map.37 = (bf16[16,33,8,128]{3,2,1,0:T(8,128)(2,1)S(1)}, s32[8,128]{1,0:T(8,128)S(1)}) custom-call(f32[128,1024]{1,0:T(8,128)} %rows_hbm.1, s32[1,128]{1,0:T(1,128)} %bitcast.21, s32[1,128]{1,0:T(1,128)} %bitcast.22), custom_call_target="tpu_custom_call" | custom-call | flops 134217728 | bytes 1605632 | tf_op jit(solution)/shard_map/pallas_call | solution.py:245
  1.7 0.8 %conditional.5 = (bf16[64,33,2,128]{3,2,1,0:T(2,128)(2,1)S(1)}) conditional(s32[]{:T(128)} %convert_element_type.8, bf16[64,33,2,128]{3,2,1,0:T(2,128)(2,1)S(1)} %bitcast.11, bf16[64,33,2,128]{3,2,1,0:T(2,128)(2,1)S(1)} %bitcast.12), branch_computations={%region_2.0_spmd, %region_3.0_spmd} | conditional | bytes 2162696 | solution.py:266
  1.7 0.7 %copy.6 = bf16[64,33,2,128]{3,2,1,0:T(2,128)(2,1)S(1)} copy(bf16[64,33,2,128]{3,2,1,0:T(2,128)(2,1)S(1)} %param.2) | data formatting | bytes 2162688 | tf_op jit(solution)/shard_map/cond
  2.5 1.3 %collective-permute-start = (bf16[1040,512]{1,0:T(8,128)(2,1)S(1)}, bf16[1040,512]{1,0:T(8,128)(2,1)S(1)}, u32[]{:S(2)}, u32[]{:S(2)}) collective-permute-start(bf16[1040,512]{1,0:T(8,128)(2,1)S(1)} %shard_map.38.mine_ref), channel_id=1, source_target_pairs={{4,0},{5,1},{6,2},{7,3},{12,8},{13,9},{14,10},{15,11},{20,16},{21,... | collective-permute-start | bytes 3194888 | tf_op jit(solution)/shard_map/ppermute | solution.py:273
  3.8 28.1 %conditional.4 = (bf16[64,33,2,128]{3,2,1,0:T(2,128)(2,1)S(1)}) conditional(s32[]{:T(128)} %convert_element_type.9, bf16[64,33,2,128]{3,2,1,0:T(2,128)(2,1)S(1)} %bitcast.13, bf16[64,33,2,128]{3,2,1,0:T(2,128)(2,1)S(1)} %bitcast.14), branch_computations={%region_0.0_spmd, %region_1.0_spmd} | conditional | bytes 4325384 | solution.py:267
  3.8 0.7 %copy.12 = bf16[64,33,2,128]{3,2,1,0:T(2,128)(2,1)S(1)} copy(bf16[64,33,2,128]{3,2,1,0:T(2,128)(2,1)S(1)} %param.1) | data formatting | bytes 2162688 | tf_op jit(solution)/shard_map/cond
  4.5 27.3 %all_to_all.26 = bf16[64,33,2,128]{3,2,1,0:T(2,128)(2,1)S(1)} all-to-all(bf16[64,33,2,128]{3,2,1,0:T(2,128)(2,1)S(1)} %copy.12), channel_id=1, replica_groups=mesh['zy'=16,'core'=2,'x'=4] {'x','zy'}, dimensions={0} | all-to-all | bytes 2162688 | tf_op jit(solution)/shard_map/cond/branch_1_fun/all_to_all | solution.py:260
  31.9 0.0 collective-permute-done.other_ref
  31.9 0.8 %shard_map.39 = (f32[512,128]{1,0:T(8,128)S(1)}, f32[8,512]{1,0:T(8,128)S(1)}) custom-call(bf16[16,33,8,128]{3,2,1,0:T(8,128)(2,1)S(1)} %bitcast.15, bf16[1040,512]{1,0:T(8,128)(2,1)S(1)} %collective-permute-done.other_ref), custom_call_target="tpu_custom_call" | custom-call | flops 536870912 | bytes 2162688 | tf_op jit(solution)/shard_map/pallas_call | solution.py:274
  32.7 0.1 collective-permute-start.1
  32.8 0.8 %shard_map.40 = (f32[64,128]{1,0:T(8,128)S(1)}, f32[8,512]{1,0:T(8,128)S(1)}) custom-call(bf16[16,33,8,128]{3,2,1,0:T(8,128)(2,1)S(1)} %bitcast.16, f32[512,128]{1,0:T(8,128)S(1)} %get-tuple-element.38.cross_ref, bf16[1040,512]{1,0:T(8,128)(2,1)S(1)} %shard_map.38.mine_ref), custom_call_target="tpu_custom_call" | custom-call | flops 536870912 | bytes 2162688 | tf_op jit(solution)/shard_map/pallas_call | solution.py:280
  33.5 14.3 %conditional.6 = (f32[64,128]{1,0:T(8,128)S(1)}) conditional(s32[]{:T(128)} %convert_element_type.9, f32[64,128]{1,0:T(8,128)S(1)} %get-tuple-element.39, f32[64,128]{1,0:T(8,128)S(1)} %get-tuple-element.39), branch_computations={%region_4.0_spmd, %region_5.0_spmd} | conditional | bytes 131080 | solution.py:281
  33.6 14.2 %all_to_all.28 = f32[64,1,128]{2,1,0:T(1,128)S(1)} all-to-all(f32[64,1,128]{2,1,0:T(1,128)S(1)} %copy.13), channel_id=1, replica_groups=mesh['zy'=16,'core'=2,'x'=4] {'x','zy'}, dimensions={0} | all-to-all | bytes 65536 | tf_op jit(solution)/shard_map/cond/branch_1_fun/all_to_all | solution.py:260
  47.8 0.0 collective-permute-done.1.away_ref
  47.8 0.7 %shard_map.42 = f32[1,128]{1,0:T(1,128)} custom-call(f32[64,128]{1,0:T(8,128)S(1)} %get-tuple-element.49.best_ref, s32[8,128]{1,0:T(8,128)S(1)} %get-tuple-element.42.where_ref), custom_call_target="tpu_custom_call" | custom-call | bytes 32768 | tf_op jit(solution)/shard_map/pallas_call | solution.py:284
  (4 shorter events, 0.0 us)
Async XLA Ops:
  2.5 29.4 %collective-permute-start = (bf16[1040,512]{1,0:T(8,128)(2,1)S(1)}, bf16[1040,512]{1,0:T(8,128)(2,1)S(1)}, u32[]{:S(2)}, u32[]{:S(2)}) collective-permute-start(bf16[1040,512]{1,0:T(8,128)(2,1)S(1)} %shard_map.38.mine_ref), channel_id=1, source_target_pairs={{4,0},{5,1},{6,2},{7,3},{12,8},{13,9},{14,10},{15,11},{20,16},{21,... | collective-permute-start | bytes 3194888 | tf_op jit(solution)/shard_map/ppermute | solution.py:273
  32.7 15.1 %collective-permute-start.1 = (f32[8,512]{1,0:T(8,128)S(1)}, f32[8,512]{1,0:T(8,128)S(1)}, u32[]{:S(2)}, u32[]{:S(2)}) collective-permute-start(f32[8,512]{1,0:T(8,128)S(1)} %get-tuple-element.41), channel_id=1, source_target_pairs={{0,4},{4,0},{1,5},{5,1},{2,6},{6,2},{3,7},{7,3},{8,12},{12,8},{9,1... | collective-permute-start | bytes 49160 | tf_op jit(solution)/shard_map/ppermute | solution.py:277

commit v5 on v4

--- a/solution.py
+++ b/solution.py
@@ -111,7 +111,7 @@
 
 
 def similarities(keys, queries_ref):
-    step = 2 * LANES
+    step = 4 * LANES
     for at in range(0, queries_ref.shape[1], step):
         similar = jnp.dot(
             keys, queries_ref[: keys.shape[1], at : at + step], preferred_element_type=jnp.float32
@@ -176,7 +176,7 @@
         cross = largest(cross_ref[...].T)
         line = ranks.T[0:1]
         best = []
-        step = 2 * LANES
+        step = 4 * LANES
         for at in range(0, rows.shape[0], step):
             similar = lax.dot_general(
                 rows, rows[at : at + step], NT, preferred_element_type=jnp.float32
@@ -192,7 +192,7 @@
         marks = mine_ref[width:].astype(jnp.float32)
         line = marks[0:1] * 16.0 + marks[1:2]
         ranks = jnp.broadcast_to(line, (LANES, line.shape[1])).T
-        step = 2 * LANES
+        step = 4 * LANES
         for at in range(0, line.shape[1], step):
             similar = lax.dot_general(
                 mine_ref[:width],

time: 48.7 us -> 48.7 us (level)
  no operation moved by 1% of the time
where the time goes in v5:
time: 48.7 us; the launch traced here: 48.5 us
  blocking collectives  41.5 us (85%)
  Pallas kernels  3.93 us (8%)
  local copies, waits for them, and re-layouts  1.49 us (3%)
  starting transfers between devices  1.38 us (3%)
    all_to_all x2, blocking collectives, exchange(): lax.all_to_all(sent, ('x', 'zy'), split_axis=0, concat_axis=0, tiled=True)  41.5 us
    pallas_call x1, Pallas kernels, per_device(): call(pack_kernel, (shape(tiles, bf16), shape((8, docs), i32)), 2 * slots...  1.66 us
    cond x3, local copies, waits for them, and re-layouts  1.49 us
    ppermute x1, starting transfers between devices, per_device(): other = lax.ppermute(turned, 'core', [(1, 0)])  1.29 us
  transfers between devices with their start and end apart: 2, of which 0 were waited for; matrix products, arithmetic and copies ran while one was open for 2% of the time, Pallas kernels for 2%

profile of v5, /device:TPU:0, one launch (start us, length us, event | category | flops | bytes accessed | tf_op | source)
XLA Modules:
  0.0 48.5 jit_solution(1040381358174263416)
XLA Ops:
  0.0 1.7 %shard_map.37 = (bf16[16,33,8,128]{3,2,1,0:T(8,128)(2,1)S(1)}, s32[8,128]{1,0:T(8,128)S(1)}) custom-call(f32[128,1024]{1,0:T(8,128)} %rows_hbm.1, s32[1,128]{1,0:T(1,128)} %bitcast.21, s32[1,128]{1,0:T(1,128)} %bitcast.22), custom_call_target="tpu_custom_call" | custom-call | flops 134217728 | bytes 1605632 | tf_op jit(solution)/shard_map/pallas_call | solution.py:245
  1.7 0.8 %conditional.5 = (bf16[64,33,2,128]{3,2,1,0:T(2,128)(2,1)S(1)}) conditional(s32[]{:T(128)} %convert_element_type.8, bf16[64,33,2,128]{3,2,1,0:T(2,128)(2,1)S(1)} %bitcast.11, bf16[64,33,2,128]{3,2,1,0:T(2,128)(2,1)S(1)} %bitcast.12), branch_computations={%region_2.0_spmd, %region_3.0_spmd} | conditional | bytes 2162696 | solution.py:266
  1.7 0.7 %copy.6 = bf16[64,33,2,128]{3,2,1,0:T(2,128)(2,1)S(1)} copy(bf16[64,33,2,128]{3,2,1,0:T(2,128)(2,1)S(1)} %param.2) | data formatting | bytes 2162688 | tf_op jit(solution)/shard_map/cond
  2.5 1.3 %collective-permute-start = (bf16[1040,512]{1,0:T(8,128)(2,1)S(1)}, bf16[1040,512]{1,0:T(8,128)(2,1)S(1)}, u32[]{:S(2)}, u32[]{:S(2)}) collective-permute-start(bf16[1040,512]{1,0:T(8,128)(2,1)S(1)} %shard_map.38.mine_ref), channel_id=1, source_target_pairs={{4,0},{5,1},{6,2},{7,3},{12,8},{13,9},{14,10},{15,11},{20,16},{21,... | collective-permute-start | bytes 3194888 | tf_op jit(solution)/shard_map/ppermute | solution.py:273
  3.8 28.1 %conditional.4 = (bf16[64,33,2,128]{3,2,1,0:T(2,128)(2,1)S(1)}) conditional(s32[]{:T(128)} %convert_element_type.9, bf16[64,33,2,128]{3,2,1,0:T(2,128)(2,1)S(1)} %bitcast.13, bf16[64,33,2,128]{3,2,1,0:T(2,128)(2,1)S(1)} %bitcast.14), branch_computations={%region_0.0_spmd, %region_1.0_spmd} | conditional | bytes 4325384 | solution.py:267
  3.8 0.7 %copy.12 = bf16[64,33,2,128]{3,2,1,0:T(2,128)(2,1)S(1)} copy(bf16[64,33,2,128]{3,2,1,0:T(2,128)(2,1)S(1)} %param.1) | data formatting | bytes 2162688 | tf_op jit(solution)/shard_map/cond
  4.5 27.3 %all_to_all.26 = bf16[64,33,2,128]{3,2,1,0:T(2,128)(2,1)S(1)} all-to-all(bf16[64,33,2,128]{3,2,1,0:T(2,128)(2,1)S(1)} %copy.12), channel_id=1, replica_groups=mesh['zy'=16,'core'=2,'x'=4] {'x','zy'}, dimensions={0} | all-to-all | bytes 2162688 | tf_op jit(solution)/shard_map/cond/branch_1_fun/all_to_all | solution.py:260
  31.9 0.0 collective-permute-done.other_ref
  31.9 0.8 %shard_map.39 = (f32[512,128]{1,0:T(8,128)S(1)}, f32[8,512]{1,0:T(8,128)S(1)}) custom-call(bf16[16,33,8,128]{3,2,1,0:T(8,128)(2,1)S(1)} %bitcast.15, bf16[1040,512]{1,0:T(8,128)(2,1)S(1)} %collective-permute-done.other_ref), custom_call_target="tpu_custom_call" | custom-call | flops 536870912 | bytes 2162688 | tf_op jit(solution)/shard_map/pallas_call | solution.py:274
  32.7 0.1 collective-permute-start.1
  32.8 0.8 %shard_map.40 = (f32[64,128]{1,0:T(8,128)S(1)}, f32[8,512]{1,0:T(8,128)S(1)}) custom-call(bf16[16,33,8,128]{3,2,1,0:T(8,128)(2,1)S(1)} %bitcast.16, f32[512,128]{1,0:T(8,128)S(1)} %get-tuple-element.38.cross_ref, bf16[1040,512]{1,0:T(8,128)(2,1)S(1)} %shard_map.38.mine_ref), custom_call_target="tpu_custom_call" | custom-call | flops 536870912 | bytes 2162688 | tf_op jit(solution)/shard_map/pallas_call | solution.py:280
  33.5 14.3 %conditional.6 = (f32[64,128]{1,0:T(8,128)S(1)}) conditional(s32[]{:T(128)} %convert_element_type.9, f32[64,128]{1,0:T(8,128)S(1)} %get-tuple-element.39, f32[64,128]{1,0:T(8,128)S(1)} %get-tuple-element.39), branch_computations={%region_4.0_spmd, %region_5.0_spmd} | conditional | bytes 131080 | solution.py:281
  33.6 14.2 %all_to_all.28 = f32[64,1,128]{2,1,0:T(1,128)S(1)} all-to-all(f32[64,1,128]{2,1,0:T(1,128)S(1)} %copy.13), channel_id=1, replica_groups=mesh['zy'=16,'core'=2,'x'=4] {'x','zy'}, dimensions={0} | all-to-all | bytes 65536 | tf_op jit(solution)/shard_map/cond/branch_1_fun/all_to_all | solution.py:260
  47.8 0.0 collective-permute-done.1.away_ref
  47.8 0.7 %shard_map.42 = f32[1,128]{1,0:T(1,128)} custom-call(f32[64,128]{1,0:T(8,128)S(1)} %get-tuple-element.49.best_ref, s32[8,128]{1,0:T(8,128)S(1)} %get-tuple-element.42.where_ref), custom_call_target="tpu_custom_call" | custom-call | bytes 32768 | tf_op jit(solution)/shard_map/pallas_call | solution.py:284
  (4 shorter events, 0.0 us)
Async XLA Ops:
  2.5 29.4 %collective-permute-start = (bf16[1040,512]{1,0:T(8,128)(2,1)S(1)}, bf16[1040,512]{1,0:T(8,128)(2,1)S(1)}, u32[]{:S(2)}, u32[]{:S(2)}) collective-permute-start(bf16[1040,512]{1,0:T(8,128)(2,1)S(1)} %shard_map.38.mine_ref), channel_id=1, source_target_pairs={{4,0},{5,1},{6,2},{7,3},{12,8},{13,9},{14,10},{15,11},{20,16},{21,... | collective-permute-start | bytes 3194888 | tf_op jit(solution)/shard_map/ppermute | solution.py:273
  32.7 15.1 %collective-permute-start.1 = (f32[8,512]{1,0:T(8,128)S(1)}, f32[8,512]{1,0:T(8,128)S(1)}, u32[]{:S(2)}, u32[]{:S(2)}) collective-permute-start(f32[8,512]{1,0:T(8,128)S(1)} %get-tuple-element.41), channel_id=1, source_target_pairs={{0,4},{4,0},{1,5},{5,1},{2,6},{6,2},{3,7},{7,3},{8,12},{12,8},{9,1... | collective-permute-start | bytes 49160 | tf_op jit(solution)/shard_map/ppermute | solution.py:277
